TPU v7x, 128 devices: a whole 4x4x4 slice. The times are simulated.
128 devices in a mesh: weld: 8 (over x, core), trans: 16 (over z, y).
Axes of the slice: x: 4, y: 4, z: 4, core: 2. Of those that a mesh axis runs over, the one named last changes fastest.
Arguments:
- weights: bfloat16 [49152, 64, 256], P(('weld', 'trans'))
- particle_state: float32 [10, 3145728], P(None, ('weld', 'trans')), may hold values from -6 to 6
- mass: float32 [3145728], P(('weld', 'trans')), may hold values from 0.5 to 2
- stiffness: float32 [3145728], P(('weld', 'trans')), may hold values from 1 to 10
- targets: int32 [49152], P(('weld', 'trans')), may hold values from 0 to 8191, as said below
- counts: int32 [49152], P(('weld', 'trans')), may hold values from 0 to 64, as said below
- partner_bit: int32 [128], P(('weld', 'trans')), may hold values from 0 to 1, as said below
- swap_list: int32 [128, 24], P(('weld', 'trans')), may hold values from 0 to 383, as said below
Outputs:
- particle_next: float32 [10, 3145728], P(None, ('weld', 'trans'))
- node_fields: bfloat16 [8192, 256], P(('weld', 'trans'))
Inputs may be any that keep to these rules, and one draw needn't show every extreme that they name: `partner_bit`: equal for all devices with the same trans index, so that partners agree. `swap_list`: each row holds 24 different local block indices. `targets`: node block g belongs to device g // 64. After the swap, at most 4 blocks of one device name node blocks of any one device, and exactly 4 name node blocks of the device itself. `counts`: every device has a full block.
All inputs are finite; a program needn't handle non-finite values.
Results may differ from a plain program's by a relative error of at most 0.005.
Values may be sent and summed in bfloat16 or wider, within the bound.
A program may use at most 192 MiB of HBM per device.

v0:
```python
import functools

import jax
import jax.numpy as jnp
from jax import lax
from jax.experimental import pallas as pl
from jax.experimental.pallas import tpu as pltpu
from jax.sharding import PartitionSpec as P

BS = 64
NBD = 64
PB = 384
SW = 24
N_WELD = 8
N_TRANS = 16
OWN = 128
SLOTS = 4
PAIRS = PB // 2
XPAIRS = SW // 2
ALLP = PAIRS + XPAIRS
ROWS = OWN * 2 * SLOTS
EXT = 512
SWP = 32
CHUNKS = 12
CHP = PAIRS // CHUNKS

f32 = jnp.float32
bf16 = jnp.bfloat16
MESH = pl.DeviceIdType.MESH


def iota(shape, dim):
    return lax.broadcasted_iota(jnp.int32, shape, dim)


def coords(dev):
    return (dev // N_TRANS, dev % N_TRANS)


def dot(lhs, rhs):
    return lax.dot_general(lhs, rhs, (((1,), (0,)), ((), ())), preferred_element_type=f32)


def dot_nt(lhs, rhs):
    return lax.dot_general(lhs, rhs, (((1,), (1,)), ((), ())), preferred_element_type=f32)


def weld_kernel(
    w_hbm, st_ref, mass_ref, stiff_ref, tgt_ref, cnt_ref, bit_ref, swap_ref,
    out_ref, field_ref, xout_ref,
    w_ref, s0_ref, s1_ref, m_ref, sf_ref, pt_ref, pb_ref, fbx_ref, kc_ref, kr_ref,
    sd_ref, at_ref, a_ref, ms_ref,
    send1, recv1, send2, recv2, ans_s, ans_r,
    hs1, hr1, hs2, hr2, fs, fr, xs, xr,
    wsem, asem_s, asem_r, hsem_s, hsem_r,
):
    weld = lax.axis_index("weld")
    trans = lax.axis_index("trans")
    me = weld * N_TRANS + trans
    bar = pltpu.get_barrier_semaphore()

    def chunk_copy(c):
        part = pl.ds(c * CHP * 2, CHP * 2)
        return pltpu.make_async_copy(w_hbm.at[part], w_ref.at[part], wsem.at[c])

    for c in range(CHUNKS):
        chunk_copy(c).start()

    def greet(j, carry):
        pl.semaphore_signal(
            bar, inc=1, device_id=coords(lax.rem(me + j, OWN)), device_id_type=MESH
        )
        return carry

    lax.fori_loop(1, OWN, greet, 0)

    row8 = iota((8, 128), 0)
    lane8 = iota((8, 128), 1)
    lo = lane8 < 64
    lane64 = lane8 % 64

    def all_to_all(src, dst, ph):
        dst[me] = src[me]

        def go(j, carry):
            dev = lax.rem(me + j, OWN)
            pltpu.make_async_remote_copy(
                src.at[dev], dst.at[me], asem_s.at[ph], asem_r.at[ph],
                device_id=coords(dev), device_id_type=MESH,
            ).start()
            return carry

        lax.fori_loop(1, OWN, go, 0)

    def all_to_all_wait(src, dst, ph):
        part = dst.at[pl.ds(0, OWN - 1)]
        pltpu.make_async_copy(part, part, asem_r.at[ph]).wait()
        part = src.at[pl.ds(0, OWN - 1)]
        pltpu.make_async_copy(part, part, asem_s.at[ph]).wait()

    def partner_copies(src, dst, ph):
        out = []
        for bit in range(2):
            step = 1 << bit
            other = weld + step - 2 * step * ((weld // step) % 2)
            out.append(
                pltpu.make_async_remote_copy(
                    src, dst.at[bit], hsem_s.at[ph, bit], hsem_r.at[ph, bit],
                    device_id=(other, trans), device_id_type=MESH,
                )
            )
        return out

    my_bit = bit_ref[0]

    def picked(ref):
        return jnp.where(my_bit == 0, ref[0].astype(f32), ref[1].astype(f32))

    head = row8 < 3
    blk = [lo, jnp.logical_not(lo)]
    zero8 = jnp.zeros((8, 128), f32)

    def scatter_pair(q, s0, s1, mass8):
        t0 = s0 * mass8
        t1 = s1 * (-0.25 * mass8)
        kinds = [t0, t1, pltpu.roll(t1, 3, 0), pltpu.roll(t1, 6, 0)]
        kinds = [t0] + [jnp.where(head, k, 0.0) for k in kinds[1:]]
        tiles = [[jnp.where(blk[b], kinds[k], 0.0) for k in range(4)] for b in range(2)]
        lhs_a = jnp.concatenate(
            [tiles[0][0], tiles[0][1], tiles[1][0], tiles[1][1]], 0
        ).astype(bf16)
        lhs_b = jnp.concatenate(
            [tiles[0][2], tiles[0][3], tiles[1][2], tiles[1][3]], 0
        ).astype(bf16)
        w_pair = w_ref[pl.ds(2 * q, 2)].reshape(128, 256)
        res_a = dot(lhs_a, w_pair[:, 0:128])
        res_b = dot(lhs_b, w_pair[:, 128:256])
        both = []
        for b in range(2):
            both.append(
                jnp.where(lo, res_a[b * 16 : b * 16 + 8], res_a[b * 16 + 8 : b * 16 + 16])
                + jnp.where(lo, res_b[b * 16 : b * 16 + 8], res_b[b * 16 + 8 : b * 16 + 16])
            )
        pt_ref[pl.ds(pl.multiple_of(q * 16, 16), 16), :] = jnp.concatenate(both, 0)

    def first_pair(q, carry):
        lanes = pl.ds(pl.multiple_of(q * 128, 128), 128)

        def row(r):
            return jnp.broadcast_to(st_ref[r : r + 1, lanes], (8, 128))

        s0 = jnp.where(row8 < 4, st_ref[0:8, lanes], jnp.where(row8 == 4, 1.0, 0.0))
        xy, yz = row(7), row(8)
        s1 = jnp.where(row8 == 0, row(4), xy)
        s1 = jnp.where(row8 == 2, row(9), s1)
        s1 = jnp.where(jnp.logical_or(row8 == 3, row8 == 7), yz, s1)
        s1 = jnp.where(row8 == 4, row(6), s1)
        s1 = jnp.where(row8 == 6, row(5), s1)
        many = jnp.where(lo, cnt_ref[2 * q], cnt_ref[2 * q + 1])
        live = lane64 < many
        mass8 = jnp.where(live, jnp.broadcast_to(mass_ref[0:1, lanes], (8, 128)), 0.0)
        stiff8 = jnp.where(live, 0.25 * jnp.broadcast_to(stiff_ref[0:1, lanes], (8, 128)), 0.0)
        s0_ref[q] = s0
        s1_ref[q] = s1
        m_ref[q] = mass8
        sf_ref[q] = stiff8
        scatter_pair(q, s0, s1, mass8)
        return carry

    def next_scatter(q, carry):
        scatter_pair(q, s0_ref[q], s1_ref[q], m_ref[q])
        return carry

    hi = jnp.logical_not(lo)

    def rows_in(*which):
        hit = row8 == which[0]
        for w in which[1:]:
            hit = jnp.logical_or(hit, row8 == w)
        return hit

    def mask(*terms):
        total = zero8
        for value, which, lanes in terms:
            total = total + jnp.where(jnp.logical_and(rows_in(*which), lanes), value, 0.0)
        return total

    f0h0 = [
        mask((1.0, (0,), lo)),
        mask((1.0, (2,), lo)),
        mask((1.0, (1,), lo), (1.0, (5,), hi)),
        mask((1.0, (3,), lo)),
    ]
    f0h1 = [None, None, mask((1.0, (5,), lo)), mask((1.0, (5,), hi))]
    f1h0 = [
        mask((1.0, (1, 5), hi)),
        None,
        mask((2.0, (0,), hi)),
        mask((1.0, (2,), hi)),
    ]
    f1h1 = [
        mask((1.0, (1, 5), lo), (1.0, (3, 7), hi)),
        mask((1.0, (3, 7), lo)),
        mask((2.0, (6,), lo), (1.0, (2,), hi)),
        mask((2.0, (4,), hi)),
    ]
    diag = rows_in(0, 4, 6)

    def combine(masks, vals):
        total = None
        for m, v in zip(masks, vals):
            if m is not None:
                term = m * v
                total = term if total is None else total + term
        return total

    def gather_pair(q, four, place):
        left, right = [], []
        for b in range(2):
            vals = [
                jnp.broadcast_to(
                    four[2 * place + b : 2 * place + b + 1, g * 128 : g * 128 + 128], (8, 128)
                )
                for g in range(4)
            ]
            left += [combine(f0h0, vals), combine(f1h0, vals)]
            right += [combine(f0h1, vals), combine(f1h1, vals)]
        lhs = jnp.concatenate(
            [jnp.concatenate(left, 0).astype(bf16), jnp.concatenate(right, 0).astype(bf16)], 1
        )
        res = dot_nt(lhs, w_ref[pl.ds(2 * q, 2)].reshape(128, 256))
        o0 = jnp.where(lo, res[0:8], res[16:24])
        o1 = jnp.where(lo, res[8:16], res[24:32])
        trace = jnp.where(diag, jnp.broadcast_to(o0[5:6], (8, 128)), 0.0)
        mass8 = m_ref[q]
        s0, s1 = s0_ref[q], s1_ref[q]
        s0 = jnp.where(jnp.logical_and(mass8 > 0.0, row8 < 4), o0, s0)
        s1 = s1 + sf_ref[q] * (o1 + trace)
        return s0, s1, mass8

    def by_fours(one_pair):
        def body(g, carry):
            four = fbx_ref[pl.ds(pl.multiple_of(g * 8, 8), 8), :]
            for place in range(4):
                q = 4 * g + place
                one_pair(q, *gather_pair(q, four, place))
            return carry

        return body

    @by_fours
    def middle_four(q, s0, s1, mass8):
        s0_ref[q] = s0
        s1_ref[q] = s1
        scatter_pair(q, s0, s1, mass8)

    def natural(s0, s1):
        turned = [pltpu.roll(s1, k, 0) for k in (4, 7, 2, 6, 5)]
        top = jnp.where(row8 < 4, s0, turned[0])
        top = jnp.where(row8 == 5, turned[1], top)
        top = jnp.where(row8 == 6, turned[2], top)
        top = jnp.where(row8 == 7, turned[3], top)
        low = jnp.where(row8 == 0, turned[4], turned[1])
        return top, low

    @by_fours
    def last_four(q, s0, s1, mass8):
        top, low = natural(s0, s1)
        lanes = pl.ds(pl.multiple_of(q * 128, 128), 128)
        out_ref[0:8, lanes] = top
        out_ref[8:10, lanes] = low[0:2]

    @by_fours
    def last_extra(q, s0, s1, mass8):
        top, low = natural(s0, s1)
        lanes = pl.ds(pl.multiple_of((q - PAIRS) * 128, 128), 128)
        xs[0:8, lanes] = top
        xs[8:16, lanes] = low

    pt_ref[pl.ds(ALLP * 16, (EXT // 2 - ALLP) * 16), :] = jnp.zeros(
        ((EXT // 2 - ALLP) * 16, 128), f32
    )

    def first_chunk(c, carry):
        chunk_copy(c).wait()
        return lax.fori_loop(
            0, CHP, lambda i, got: first_pair(c * CHP + i, got), carry, unroll=4
        )

    lax.fori_loop(0, CHUNKS, first_chunk, 0)

    def take_extra(i, carry):
        blk_ids = [swap_ref[0, 2 * i + b] for b in range(2)]
        for b in range(2):
            w_ref[PB + 2 * i + b] = w_ref[blk_ids[b]]
        for ref in (s0_ref, s1_ref, m_ref, sf_ref):
            vals = []
            for b in range(2):
                v = ref[lax.div(blk_ids[b], 2)]
                vals.append(jnp.where(lax.rem(blk_ids[b], 2) == b, v, pltpu.roll(v, 64, 1)))
            ref[PAIRS + i] = jnp.where(lo, vals[0], vals[1])
        return carry

    lax.fori_loop(0, XPAIRS, take_extra, 0)
    lax.fori_loop(PAIRS, ALLP, next_scatter, 0, unroll=2)

    def channels(first, count, groups):
        lo_c = iota((count, 128), 1) < 64

        def folded(c):
            v = pt_ref[pl.ds(first * 8 + c, count, stride=8), :]
            return v + pltpu.roll(v, 64, 1)

        parts = [
            jnp.where(lo_c, folded(0), folded(1)),
            jnp.where(lo_c, folded(2), folded(3)),
        ]
        if groups > 2:
            parts.append(folded(4))
        return parts

    tgt = tgt_ref[...].astype(f32)
    own_r = jnp.floor(tgt * (1.0 / NBD))
    node_r = tgt - NBD * own_r + 1.0

    sw_row = iota((SWP, 128), 0)
    sw_col = jnp.full((SWP, 128), -1, jnp.int32)
    for s in range(SW):
        sw_col = jnp.where(sw_row == s, swap_ref[0, s], sw_col)
    flags, own_h, node_h = [], 0.0, 0.0
    for j in range(3):
        hits = (sw_col == iota((SWP, 128), 1) + 128 * j).astype(f32)
        flags.append(jnp.sum(hits, 0, keepdims=True))
        own_h = own_h + jnp.sum(hits * own_r[j : j + 1], 1, keepdims=True)
        node_h = node_h + jnp.sum(hits * node_r[j : j + 1], 1, keepdims=True)
    own_h = jnp.where(sw_row < SW, jnp.broadcast_to(own_h, (SWP, 128)), -1.0)
    node_h = jnp.broadcast_to(node_h, (SWP, 128))

    parts = channels(PB, SWP, 3)
    lo_s = iota((SWP, 128), 1) < 64
    hs1[...] = jnp.concatenate(
        [parts[0], parts[1], jnp.where(lo_s, parts[2], node_h), own_h], 1
    ).astype(bf16)

    pl.semaphore_wait(bar, OWN - 1)
    hand1 = partner_copies(hs1, hr1, 0)
    for c in hand1:
        c.start()

    own_cols = []
    for j in range(3):
        lanes = slice(j * 128, j * 128 + 128)
        own_j = jnp.where(flags[j] > 0.0, -1.0, own_r[j : j + 1])
        own_b = jnp.broadcast_to(own_j, (128, 128))
        kr_ref[:, lanes] = own_b
        own_cols.append(own_b.T)
        node_c = jnp.broadcast_to(node_r[j : j + 1], (128, 128)).T
        parts = channels(j * 128, 128, 3)
        lo_b = iota((128, 128), 1) < 64
        pb_ref[lanes, :] = jnp.concatenate(
            [parts[0], parts[1], jnp.where(lo_b, parts[2], node_c)], 1
        ).astype(bf16)
    pb_ref[PB:EXT, :] = jnp.zeros((EXT - PB, 384), bf16)

    for c in hand1:
        c.wait()
    got = picked(hr1)
    pb_ref[PB : PB + SWP, :] = got[:, 0:384].astype(bf16)
    own_cols.append(jnp.concatenate([got[:, 384:512], jnp.full((96, 128), -1.0, f32)], 0))
    kr_ref[:, PB:EXT] = own_cols[3].T

    before = iota((128, 128), 1) < iota((128, 128), 0)
    for i in range(4):
        count = jnp.zeros((128, 128), f32)
        for j in range(i + 1):
            same = own_cols[i] == kr_ref[:, j * 128 : j * 128 + 128]
            if j == i:
                same = jnp.logical_and(same, before)
            count = count + jnp.where(same, 1.0, 0.0)
        rank = jnp.broadcast_to(jnp.sum(count, 1, keepdims=True), (128, 128))
        key = jnp.where(own_cols[i] >= 0.0, own_cols[i] * SLOTS + rank, -1.0)
        kc_ref[i * 128 : i * 128 + 128, :] = key
    for i in range(4):
        kr_ref[:, i * 128 : i * 128 + 128] = kc_ref[i * 128 : i * 128 + 128, :].T

    def send_rows(c, groups):
        r = iota((128, EXT), 0) + c * 128
        row_key = ((r // 8) * SLOTS + r % SLOTS).astype(f32)
        pick = jnp.where(row_key == kr_ref[...], 1.0, 0.0).astype(bf16)
        res = dot(pick, pb_ref[:, 0 : groups * 128])
        first_half = (iota((128, 128), 0) % 8) < SLOTS
        main = jnp.where(first_half, res[:, 0:128], res[:, 128:256])
        return main.reshape(16, 8, 128), res[:, 256:]

    def fill1(c, carry):
        main, extra = send_rows(c, 3)
        owners = pl.ds(pl.multiple_of(c * 16, 16), 16)
        send1[owners] = jnp.concatenate([main, extra.reshape(16, 8, 128)], 1).astype(bf16)
        return carry

    lax.fori_loop(0, 8, fill1, 0)
    all_to_all(send1, recv1, 0)

    key_lane = iota((EXT, 128), 1)
    for c in range(8):
        lane_key = (((key_lane + c * 128) // 8) * SLOTS + key_lane % SLOTS).astype(f32)
        sd_ref[:, c * 128 : c * 128 + 128] = jnp.where(
            kc_ref[...] == lane_key, 1.0, 0.0
        ).astype(bf16)

    all_to_all_wait(send1, recv1, 0)

    half0 = (iota((128, 128), 0) % 8) < SLOTS
    node_lane = (iota((128, 128), 1) - (NBD - 1)).astype(f32)

    def grid_sum1(c):
        blocks = recv1[c * 16 : c * 16 + 16].astype(f32)
        main = blocks[:, 0:8].reshape(128, 128)
        extra = blocks[:, 8:16].reshape(128, 128)
        hit = jnp.where(
            jnp.logical_and(extra == node_lane, node_lane > 0.0), 1.0, 0.0
        )
        at_ref[c * 128 : c * 128 + 128, :] = hit.astype(bf16)
        hit_t = hit.T.astype(bf16)
        a_ref[:, c * 128 : c * 128 + 128] = hit_t
        rhs = jnp.concatenate(
            [
                jnp.where(half0, main, 0.0),
                jnp.where(half0, 0.0, main),
                jnp.where(half0, extra, 0.0),
            ],
            1,
        ).astype(bf16)
        return dot(hit_t, rhs)

    def grid_sum2(c):
        main = recv2[c * 16 : c * 16 + 16].astype(f32).reshape(128, 128)
        rhs = jnp.concatenate(
            [jnp.where(half0, main, 0.0), jnp.where(half0, 0.0, main)], 1
        ).astype(bf16)
        return dot(a_ref[:, c * 128 : c * 128 + 128], rhs)

    lane_n = iota((NBD, 128), 1)
    keep0 = (lane_n % 64) >= 8
    keep1 = jnp.logical_or(lane_n >= 64, lane_n >= 8)

    def grid_fields(total, msafe):
        vel = jnp.where(keep0, total[NBD:, 0:128] / msafe, 0.0)
        rest = jnp.where(keep1, total[NBD:, 128:256] / msafe, 0.0)
        return jnp.concatenate([vel, rest], 1).astype(bf16)

    def answer(fields, dst):
        rhs = jnp.concatenate([jnp.zeros((NBD, 256), bf16), fields], 0)

        def fill(c, carry):
            rows = pl.ds(pl.multiple_of(c * 128, 128), 128)
            res = dot(at_ref[rows, :], rhs)
            main = jnp.where(half0, res[:, 0:128], res[:, 128:256])
            owners = pl.ds(pl.multiple_of(c * 16, 16), 16)
            dst[owners] = main.reshape(16, 8, 128).astype(bf16)
            return carry

        lax.fori_loop(0, 8, fill, 0)

    def spread(src, ph):
        total = jnp.zeros((EXT, 256), f32)
        for c in range(4):
            main = src[c * 32 : c * 32 + 32].astype(f32).reshape(256, 128)
            first_half = (iota((256, 128), 0) % 8) < SLOTS
            rhs = jnp.concatenate(
                [jnp.where(first_half, main, 0.0), jnp.where(first_half, 0.0, main)], 1
            ).astype(bf16)
            total = total + dot(sd_ref[:, c * 256 : c * 256 + 256], rhs)
        fs[ph] = total[PB : PB + SWP].astype(bf16)
        copies = partner_copies(fs.at[ph], fr.at[ph], 1 + ph)
        for c in copies:
            c.start()
        fbx_ref[0:PB, 0:256] = total[0:PB]
        fbx_ref[0:PB, 256:384] = pltpu.roll(total[0:PB, 0:128], 64, 1)
        fbx_ref[0:PB, 384:512] = pltpu.roll(total[0:PB, 128:256], 64, 1)
        return copies

    def spread_end(copies, ph):
        for c in copies:
            c.wait()
        got = picked(fr.at[ph])
        fbx_ref[PB : PB + SWP, 0:256] = got
        fbx_ref[PB : PB + SWP, 256:384] = pltpu.roll(got[:, 0:128], 64, 1)
        fbx_ref[PB : PB + SWP, 384:512] = pltpu.roll(got[:, 128:256], 64, 1)

    total = grid_sum1(0)
    for c in range(1, 8):
        total = total + grid_sum1(c)
    mass_n = total[NBD:, 256:384]
    msafe = jnp.maximum(jnp.where(lane_n < 64, mass_n, pltpu.roll(mass_n, 64, 1)), 0.25)
    ms_ref[...] = msafe
    answer(grid_fields(total, msafe), ans_s.at[0])
    all_to_all(ans_s.at[0], ans_r.at[0], 1)
    all_to_all_wait(ans_s.at[0], ans_r.at[0], 1)

    copies = spread(ans_r.at[0], 0)
    lax.fori_loop(0, 24, middle_four, 0)
    spread_end(copies, 0)
    lax.fori_loop(PAIRS // 4, ALLP // 4, middle_four, 0)
    hs2[...] = jnp.concatenate(channels(PB, SWP, 2), 1).astype(bf16)
    hand2 = partner_copies(hs2, hr2, 3)
    for c in hand2:
        c.start()
    lax.fori_loop(24, PAIRS // 4, middle_four, 0)
    for j in range(3):
        pb_ref[j * 128 : j * 128 + 128, 0:256] = jnp.concatenate(
            channels(j * 128, 128, 2), 1
        ).astype(bf16)
    for c in hand2:
        c.wait()
    pb_ref[PB : PB + SWP, 0:256] = picked(hr2).astype(bf16)

    def fill2(c, carry):
        main, _ = send_rows(c, 2)
        send2[pl.ds(pl.multiple_of(c * 16, 16), 16)] = main.astype(bf16)
        return carry

    lax.fori_loop(0, 8, fill2, 0)
    all_to_all(send2, recv2, 2)
    all_to_all_wait(send2, recv2, 2)
    total = grid_sum2(0)
    for c in range(1, 8):
        total = total + grid_sum2(c)
    fields = grid_fields(total, ms_ref[...])
    field_ref[...] = fields
    answer(fields, ans_s.at[1])
    all_to_all(ans_s.at[1], ans_r.at[1], 3)
    all_to_all_wait(ans_s.at[1], ans_r.at[1], 3)

    copies = spread(ans_r.at[1], 1)
    lax.fori_loop(0, 24, last_four, 0)
    spread_end(copies, 1)
    lax.fori_loop(PAIRS // 4, ALLP // 4, last_extra, 0)
    hand3 = partner_copies(xs, xr, 4)
    for c in hand3:
        c.start()
    lax.fori_loop(24, PAIRS // 4, last_four, 0)
    for c in hand3:
        c.wait()
    xout_ref[...] = picked(xr)


def weld_call(weights, state, mass, stiff, targets, counts, bit, swap):
    vmem = pl.BlockSpec(memory_space=pltpu.VMEM)
    smem = pl.BlockSpec(memory_space=pltpu.SMEM)
    dma = pltpu.SemaphoreType.DMA
    return pl.pallas_call(
        weld_kernel,
        out_shape=(
            jax.ShapeDtypeStruct((10, PB * BS), f32),
            jax.ShapeDtypeStruct((NBD, 4 * BS), bf16),
            jax.ShapeDtypeStruct((16, XPAIRS * 128), f32),
        ),
        in_specs=[pl.BlockSpec(memory_space=pl.ANY), vmem, vmem, vmem, vmem, smem, smem, smem],
        out_specs=(vmem, vmem, vmem),
        scratch_shapes=[
            pltpu.VMEM((2 * ALLP, BS, 4 * BS), bf16),
            pltpu.VMEM((ALLP, 8, 128), f32),
            pltpu.VMEM((ALLP, 8, 128), f32),
            pltpu.VMEM((ALLP, 8, 128), f32),
            pltpu.VMEM((ALLP, 8, 128), f32),
            pltpu.VMEM((EXT * 8, 128), f32),
            pltpu.VMEM((EXT, 384), bf16),
            pltpu.VMEM((EXT, 512), f32),
            pltpu.VMEM((EXT, 128), f32),
            pltpu.VMEM((128, EXT), f32),
            pltpu.VMEM((EXT, ROWS), bf16),
            pltpu.VMEM((ROWS, 128), bf16),
            pltpu.VMEM((128, ROWS), bf16),
            pltpu.VMEM((NBD, 128), f32),
            pltpu.VMEM((OWN, 16, 128), bf16),
            pltpu.VMEM((OWN, 16, 128), bf16),
            pltpu.VMEM((OWN, 8, 128), bf16),
            pltpu.VMEM((OWN, 8, 128), bf16),
            pltpu.VMEM((2, OWN, 8, 128), bf16),
            pltpu.VMEM((2, OWN, 8, 128), bf16),
            pltpu.VMEM((SWP, 512), bf16),
            pltpu.VMEM((2, SWP, 512), bf16),
            pltpu.VMEM((SWP, 256), bf16),
            pltpu.VMEM((2, SWP, 256), bf16),
            pltpu.VMEM((2, SWP, 256), bf16),
            pltpu.VMEM((2, 2, SWP, 256), bf16),
            pltpu.VMEM((16, XPAIRS * 128), f32),
            pltpu.VMEM((2, 16, XPAIRS * 128), f32),
            dma((CHUNKS,)),
            dma((4,)),
            dma((4,)),
            dma((5, 2)),
            dma((5, 2)),
        ],
        compiler_params=pltpu.CompilerParams(
            collective_id=0, has_side_effects=True, vmem_limit_bytes=56 * 1024 * 1024
        ),
    )(weights, state, mass, stiff, targets, counts, bit, swap)


def place_kernel(own_ref, got_ref, swap_ref, out_ref):
    out_ref[...] = own_ref[...]
    lane = iota((8, 128), 1)

    def place(s, carry):
        blk_id = swap_ref[0, s]
        src = pl.ds(pl.multiple_of((s // 2) * 128, 128), 128)
        dst = pl.ds(pl.multiple_of((blk_id // 2) * 128, 128), 128)
        same = (s % 2) == (blk_id % 2)
        mine = (lane >= 64) == (blk_id % 2 == 1)
        top, low = got_ref[0:8, src], got_ref[8:16, src]
        top = jnp.where(same, top, pltpu.roll(top, 64, 1))
        low = jnp.where(same, low, pltpu.roll(low, 64, 1))
        out_ref[0:8, dst] = jnp.where(mine, top, out_ref[0:8, dst])
        out_ref[8:10, dst] = jnp.where(mine[0:2], low[0:2], out_ref[8:10, dst])
        return carry

    lax.fori_loop(0, SW, place, 0)


def place_call(own, got, swap):
    vmem = pl.BlockSpec(memory_space=pltpu.VMEM)
    return pl.pallas_call(
        place_kernel,
        out_shape=jax.ShapeDtypeStruct((10, PB * BS), f32),
        in_specs=[vmem, vmem, pl.BlockSpec(memory_space=pltpu.SMEM)],
        out_specs=vmem,
        compiler_params=pltpu.CompilerParams(vmem_limit_bytes=32 * 1024 * 1024),
    )(own, got, swap)


def shards(weights, particle_state, mass, stiffness, targets, counts, partner_bit, swap_list):
    own, fields, got = weld_call(
        weights,
        particle_state,
        mass.reshape(1, PB * BS),
        stiffness.reshape(1, PB * BS),
        targets.reshape(3, 128),
        counts,
        partner_bit,
        swap_list,
    )
    return place_call(own, got, swap_list), fields


def solution(mesh):
    both = ("weld", "trans")
    in_specs = (
        P(both, None, None),
        P(None, both),
        P(both),
        P(both),
        P(both),
        P(both),
        P(both),
        P(both, None),
    )
    out_specs = (P(None, both), P(both, None))
    return jax.shard_map(shards, mesh=mesh, in_specs=in_specs, out_specs=out_specs, check_vma=False)
```

profile of v0, /device:TPU:1, one launch (start us, length us, event | category | flops | bytes accessed | tf_op | source)
XLA Modules:
  0.0 105.4 jit_solution(14876526998975969572)
XLA Ops:
  1.3 0.0 copy-start.2
  1.3 97.6 %shard_map.95 = (f32[10,24576]{1,0:T(8,128)}, bf16[64,256]{1,0:T(8,128)(2,1)}, f32[16,1536]{1,0:T(8,128)}) custom-call(bf16[384,64,256]{2,1,0:T(8,128)(2,1)} %w_hbm.1, f32[10,24576]{1,0:T(8,128)} %st_ref.1, f32[1,24576]{1,0:T(1,128)} %bitcast.3, f32[1,24576]{1,0:T(1,128)} %bitcast.4, s32[3,128]{1,0:T(4,128)} %bitcast.5, s32[384]{0:T(512)} %cnt_ref.1, ...), custom_call_target="tpu_custom_call" | custom-call | tf_op jit(solution)/shard_map/pallas_call | solution.py:552
  98.9 0.0 copy-done.2
  98.9 0.0 copy-start
  98.9 1.4 %copy-done = f32[10,24576]{1,0:T(8,128)S(1)} copy-done((f32[10,24576]{1,0:T(8,128)S(1)}, f32[10,24576]{1,0:T(8,128)}, u32[]{:S(2)}) %copy-start) | copy-done | bytes 983064
  100.3 0.0 copy-start.1
  100.3 0.9 copy-done.1
  101.2 0.0 copy-start.3
  101.2 3.5 %shard_map.96 = f32[10,24576]{1,0:T(8,128)} custom-call(f32[10,24576]{1,0:T(8,128)S(1)} %copy-done, f32[16,1536]{1,0:T(8,128)S(1)} %copy-done.1, s32[1,24]{1,0:T(1,128)S(1)} %copy-done.2), custom_call_target="tpu_custom_call" | custom-call | tf_op jit(solution)/shard_map/pallas_call | solution.py:624
  104.7 0.0 copy-done.3
  104.7 0.6 copy.12
Async XLA Ops:
  1.3 97.6 %copy-start.2 = (s32[1,24]{1,0:T(1,128)S(1)}, s32[1,24]{1,0:T(1,128)}, u32[]{:S(2)}) copy-start(s32[1,24]{1,0:T(1,128)} %swap_ref.3) | copy-start | bytes 292
  98.9 1.4 %copy-start = (f32[10,24576]{1,0:T(8,128)S(1)}, f32[10,24576]{1,0:T(8,128)}, u32[]{:S(2)}) copy-start(f32[10,24576]{1,0:T(8,128)} %get-tuple-element.5.own_ref) | copy-start | bytes 2949124
  100.3 0.9 copy-start.1
  101.2 3.5 %copy-start.3 = (bf16[64,256]{1,0:T(8,128)(2,1)S(1)}, bf16[64,256]{1,0:T(8,128)(2,1)}, u32[]{:S(2)}) copy-start(bf16[64,256]{1,0:T(8,128)(2,1)} %get-tuple-element.11) | copy-start | bytes 98308
where the time goes:
time: 106 us; the launch traced here: 105 us
  Pallas kernels  101 us (95%)
  local copies, waits for them, and re-layouts  2.92 us (3%)
  between operations  1.31 us (1%)
    pallas_call x1, Pallas kernels, weld_call(): pl.pallas_call(weld_kernel, out_shape=(jax.ShapeDtypeStruct((10, PB * BS)...  97.6 us
    pallas_call x1, Pallas kernels, place_call(): pl.pallas_call(place_kernel, out_shape=jax.ShapeDtypeStruct((10, PB * BS)...  3.54 us
    unnamed x9, local copies, waits for them, and re-layouts  2.92 us

commit v1 on v0

--- a/solution.py
+++ b/solution.py
@@ -21,8 +21,11 @@
 ROWS = OWN * 2 * SLOTS
 EXT = 512
 SWP = 32
-CHUNKS = 12
-CHP = PAIRS // CHUNKS
+GROUP = 12
+CHP = 12
+CHUNKS = PAIRS // CHP
+NAT = PAIRS // GROUP
+EARLY = CHUNKS * 2 // 3
 
 f32 = jnp.float32
 bf16 = jnp.bfloat16
@@ -48,7 +51,7 @@
 def weld_kernel(
     w_hbm, st_ref, mass_ref, stiff_ref, tgt_ref, cnt_ref, bit_ref, swap_ref,
     out_ref, field_ref, xout_ref,
-    w_ref, s0_ref, s1_ref, m_ref, sf_ref, pt_ref, pb_ref, fbx_ref, kc_ref, kr_ref,
+    w_ref, s0_ref, s1_ref, m0_ref, m1_ref, f0_ref, f1_ref, pt_ref, pb_ref, fbx_ref, kc_ref, kr_ref,
     sd_ref, at_ref, a_ref, ms_ref,
     send1, recv1, send2, recv2, ans_s, ans_r,
     hs1, hr1, hs2, hr2, fs, fr, xs, xr,
@@ -78,19 +81,31 @@
     lane8 = iota((8, 128), 1)
     lo = lane8 < 64
     lane64 = lane8 % 64
-
-    def all_to_all(src, dst, ph):
+    gap = jnp.logical_or(row8 == 3, row8 == 4)
+
+    def all_to_all(fill, src, dst, ph):
+        def row(i, carry):
+            w = lax.rem(weld + i, N_WELD)
+            fill(w)
+
+            def go(j, inner):
+                t = lax.rem(trans + j, N_TRANS)
+                dev = w * N_TRANS + t
+
+                @pl.when(dev != me)
+                def _():
+                    pltpu.make_async_remote_copy(
+                        src.at[dev], dst.at[me], asem_s.at[ph], asem_r.at[ph],
+                        device_id=(w, t), device_id_type=MESH,
+                    ).start()
+
+                return inner
+
+            lax.fori_loop(0, N_TRANS, go, 0)
+            return carry
+
+        lax.fori_loop(0, N_WELD, row, 0)
         dst[me] = src[me]
-
-        def go(j, carry):
-            dev = lax.rem(me + j, OWN)
-            pltpu.make_async_remote_copy(
-                src.at[dev], dst.at[me], asem_s.at[ph], asem_r.at[ph],
-                device_id=coords(dev), device_id_type=MESH,
-            ).start()
-            return carry
-
-        lax.fori_loop(1, OWN, go, 0)
 
     def all_to_all_wait(src, dst, ph):
         part = dst.at[pl.ds(0, OWN - 1)]
@@ -116,59 +131,47 @@
     def picked(ref):
         return jnp.where(my_bit == 0, ref[0].astype(f32), ref[1].astype(f32))
 
-    head = row8 < 3
-    blk = [lo, jnp.logical_not(lo)]
-    zero8 = jnp.zeros((8, 128), f32)
-
-    def scatter_pair(q, s0, s1, mass8):
-        t0 = s0 * mass8
-        t1 = s1 * (-0.25 * mass8)
-        kinds = [t0, t1, pltpu.roll(t1, 3, 0), pltpu.roll(t1, 6, 0)]
-        kinds = [t0] + [jnp.where(head, k, 0.0) for k in kinds[1:]]
-        tiles = [[jnp.where(blk[b], kinds[k], 0.0) for k in range(4)] for b in range(2)]
-        lhs_a = jnp.concatenate(
-            [tiles[0][0], tiles[0][1], tiles[1][0], tiles[1][1]], 0
-        ).astype(bf16)
-        lhs_b = jnp.concatenate(
-            [tiles[0][2], tiles[0][3], tiles[1][2], tiles[1][3]], 0
-        ).astype(bf16)
+    def scatter_pair(q, s0, s1):
+        t0, t1 = s0 * m0_ref[q], s1 * m1_ref[q]
+        lhs = [
+            jnp.concatenate([jnp.where(lo, t, 0.0), jnp.where(lo, 0.0, t)], 0).astype(bf16)
+            for t in (t0, t1)
+        ]
         w_pair = w_ref[pl.ds(2 * q, 2)].reshape(128, 256)
-        res_a = dot(lhs_a, w_pair[:, 0:128])
-        res_b = dot(lhs_b, w_pair[:, 128:256])
-        both = []
-        for b in range(2):
-            both.append(
-                jnp.where(lo, res_a[b * 16 : b * 16 + 8], res_a[b * 16 + 8 : b * 16 + 16])
-                + jnp.where(lo, res_b[b * 16 : b * 16 + 8], res_b[b * 16 + 8 : b * 16 + 16])
-            )
-        pt_ref[pl.ds(pl.multiple_of(q * 16, 16), 16), :] = jnp.concatenate(both, 0)
-
-    def first_pair(q, carry):
+        return dot(lhs[0], w_pair[:, 0:128]) + dot(lhs[1], w_pair[:, 128:256])
+
+    def scatter_put(q, res):
+        pt_ref[pl.ds(pl.multiple_of(q * 16, 16), 16), :] = res
+
+    def build_pair(q, carry):
         lanes = pl.ds(pl.multiple_of(q * 128, 128), 128)
 
         def row(r):
             return jnp.broadcast_to(st_ref[r : r + 1, lanes], (8, 128))
 
-        s0 = jnp.where(row8 < 4, st_ref[0:8, lanes], jnp.where(row8 == 4, 1.0, 0.0))
-        xy, yz = row(7), row(8)
-        s1 = jnp.where(row8 == 0, row(4), xy)
-        s1 = jnp.where(row8 == 2, row(9), s1)
-        s1 = jnp.where(jnp.logical_or(row8 == 3, row8 == 7), yz, s1)
-        s1 = jnp.where(row8 == 4, row(6), s1)
-        s1 = jnp.where(row8 == 6, row(5), s1)
+        xy, yz, xz = row(7), row(8), row(9)
+        s0 = jnp.where(row8 < 4, st_ref[0:8, lanes], jnp.where(row8 == 4, 1.0, xz))
+        s0 = jnp.where(row8 == 5, row(4), jnp.where(row8 == 6, xy, s0))
+        s1 = jnp.where(row8 == 0, xy, jnp.where(row8 == 1, row(5), yz))
+        s1 = jnp.where(row8 == 5, xz, jnp.where(row8 == 7, row(6), s1))
+        s1 = jnp.where(gap, 0.0, s1)
         many = jnp.where(lo, cnt_ref[2 * q], cnt_ref[2 * q + 1])
         live = lane64 < many
         mass8 = jnp.where(live, jnp.broadcast_to(mass_ref[0:1, lanes], (8, 128)), 0.0)
         stiff8 = jnp.where(live, 0.25 * jnp.broadcast_to(stiff_ref[0:1, lanes], (8, 128)), 0.0)
         s0_ref[q] = s0
         s1_ref[q] = s1
-        m_ref[q] = mass8
-        sf_ref[q] = stiff8
-        scatter_pair(q, s0, s1, mass8)
+        m0_ref[q] = jnp.where(row8 < 5, mass8, -0.25 * mass8)
+        m1_ref[q] = -0.25 * mass8
+        f0_ref[q] = jnp.where(row8 < 5, 0.0, stiff8)
+        f1_ref[q] = jnp.where(gap, 0.0, stiff8)
         return carry
 
-    def next_scatter(q, carry):
-        scatter_pair(q, s0_ref[q], s1_ref[q], m_ref[q])
+    def scatter_group(g, carry):
+        group = [GROUP * g + p for p in range(GROUP)]
+        sums = [scatter_pair(q, s0_ref[q], s1_ref[q]) for q in group]
+        for q, res in zip(group, sums):
+            scatter_put(q, res)
         return carry
 
     hi = jnp.logical_not(lo)
@@ -180,31 +183,30 @@
         return hit
 
     def mask(*terms):
-        total = zero8
+        total = jnp.zeros((8, 128), f32)
         for value, which, lanes in terms:
             total = total + jnp.where(jnp.logical_and(rows_in(*which), lanes), value, 0.0)
         return total
 
     f0h0 = [
-        mask((1.0, (0,), lo)),
+        mask((1.0, (0,), lo), (1.0, (6,), hi)),
         mask((1.0, (2,), lo)),
-        mask((1.0, (1,), lo), (1.0, (5,), hi)),
-        mask((1.0, (3,), lo)),
+        mask((1.0, (1,), lo), (2.0, (5,), hi)),
+        mask((1.0, (3,), lo), (1.0, (7,), hi)),
     ]
-    f0h1 = [None, None, mask((1.0, (5,), lo)), mask((1.0, (5,), hi))]
+    f0h1 = [mask((1.0, (6,), lo)), None, mask((1.0, (7,), hi)), None]
     f1h0 = [
-        mask((1.0, (1, 5), hi)),
+        mask((1.0, (0,), hi)),
         None,
-        mask((2.0, (0,), hi)),
-        mask((1.0, (2,), hi)),
+        mask((1.0, (3,), hi)),
+        mask((1.0, (5,), hi)),
     ]
     f1h1 = [
-        mask((1.0, (1, 5), lo), (1.0, (3, 7), hi)),
-        mask((1.0, (3, 7), lo)),
-        mask((2.0, (6,), lo), (1.0, (2,), hi)),
-        mask((2.0, (4,), hi)),
+        mask((1.0, (0,), lo), (1.0, (2, 6), hi)),
+        mask((1.0, (2, 6), lo)),
+        mask((2.0, (1,), lo), (1.0, (3,), lo), (1.0, (5,), hi)),
+        mask((1.0, (3,), hi), (2.0, (7,), hi)),
     ]
-    diag = rows_in(0, 4, 6)
 
     def combine(masks, vals):
         total = None
@@ -214,14 +216,11 @@
                 total = term if total is None else total + term
         return total
 
-    def gather_pair(q, four, place):
+    def gather_pair(q):
         left, right = [], []
         for b in range(2):
             vals = [
-                jnp.broadcast_to(
-                    four[2 * place + b : 2 * place + b + 1, g * 128 : g * 128 + 128], (8, 128)
-                )
-                for g in range(4)
+                jnp.broadcast_to(fbx_ref[2 * q + b, g : g + 1, :], (8, 128)) for g in range(4)
             ]
             left += [combine(f0h0, vals), combine(f1h0, vals)]
             right += [combine(f0h1, vals), combine(f1h1, vals)]
@@ -231,51 +230,47 @@
         res = dot_nt(lhs, w_ref[pl.ds(2 * q, 2)].reshape(128, 256))
         o0 = jnp.where(lo, res[0:8], res[16:24])
         o1 = jnp.where(lo, res[8:16], res[24:32])
-        trace = jnp.where(diag, jnp.broadcast_to(o0[5:6], (8, 128)), 0.0)
-        mass8 = m_ref[q]
+        trace = jnp.broadcast_to(o1[3:4], (8, 128))
         s0, s1 = s0_ref[q], s1_ref[q]
-        s0 = jnp.where(jnp.logical_and(mass8 > 0.0, row8 < 4), o0, s0)
-        s1 = s1 + sf_ref[q] * (o1 + trace)
-        return s0, s1, mass8
-
-    def by_fours(one_pair):
+        fresh = jnp.logical_and(m0_ref[q] > 0.0, row8 < 4)
+        s0 = jnp.where(fresh, o0, s0 + f0_ref[q] * jnp.where(row8 == 5, o0 + trace, o0))
+        s1 = s1 + f1_ref[q] * jnp.where(
+            jnp.logical_or(row8 == 1, row8 == 7), o1 + trace, o1
+        )
+        return s0, s1
+
+    def middle_group(g, carry):
+        group = [GROUP * g + p for p in range(GROUP)]
+        state = [gather_pair(q) for q in group]
+        sums = [scatter_pair(q, *st) for q, st in zip(group, state)]
+        for q, (s0, s1), res in zip(group, state, sums):
+            s0_ref[q] = s0
+            s1_ref[q] = s1
+            scatter_put(q, res)
+        return carry
+
+    def natural(s0, s1):
+        top = jnp.where(row8 < 4, s0, pltpu.roll(s0, 7, 0))
+        top = jnp.where(row8 == 5, pltpu.roll(s1, 4, 0), top)
+        top = jnp.where(row8 == 6, pltpu.roll(s1, 7, 0), top)
+        top = jnp.where(row8 == 7, pltpu.roll(s0, 1, 0), top)
+        low = jnp.where(row8 == 0, pltpu.roll(s1, 6, 0), pltpu.roll(s0, 2, 0))
+        return top, low
+
+    def last_tiles(first, dst):
         def body(g, carry):
-            four = fbx_ref[pl.ds(pl.multiple_of(g * 8, 8), 8), :]
-            for place in range(4):
-                q = 4 * g + place
-                one_pair(q, *gather_pair(q, four, place))
+            group = [GROUP * g + p for p in range(GROUP)]
+            state = [natural(*gather_pair(q)) for q in group]
+            for q, (top, low) in zip(group, state):
+                lanes = pl.ds(pl.multiple_of((q - first) * 128, 128), 128)
+                dst[0:8, lanes] = top
+                dst[8:10, lanes] = low[0:2]
             return carry
 
         return body
 
-    @by_fours
-    def middle_four(q, s0, s1, mass8):
-        s0_ref[q] = s0
-        s1_ref[q] = s1
-        scatter_pair(q, s0, s1, mass8)
-
-    def natural(s0, s1):
-        turned = [pltpu.roll(s1, k, 0) for k in (4, 7, 2, 6, 5)]
-        top = jnp.where(row8 < 4, s0, turned[0])
-        top = jnp.where(row8 == 5, turned[1], top)
-        top = jnp.where(row8 == 6, turned[2], top)
-        top = jnp.where(row8 == 7, turned[3], top)
-        low = jnp.where(row8 == 0, turned[4], turned[1])
-        return top, low
-
-    @by_fours
-    def last_four(q, s0, s1, mass8):
-        top, low = natural(s0, s1)
-        lanes = pl.ds(pl.multiple_of(q * 128, 128), 128)
-        out_ref[0:8, lanes] = top
-        out_ref[8:10, lanes] = low[0:2]
-
-    @by_fours
-    def last_extra(q, s0, s1, mass8):
-        top, low = natural(s0, s1)
-        lanes = pl.ds(pl.multiple_of((q - PAIRS) * 128, 128), 128)
-        xs[0:8, lanes] = top
-        xs[8:16, lanes] = low
+    last_group = last_tiles(0, out_ref)
+    last_extra = last_tiles(PAIRS, xs)
 
     pt_ref[pl.ds(ALLP * 16, (EXT // 2 - ALLP) * 16), :] = jnp.zeros(
         ((EXT // 2 - ALLP) * 16, 128), f32
@@ -284,16 +279,19 @@
     def first_chunk(c, carry):
         chunk_copy(c).wait()
         return lax.fori_loop(
-            0, CHP, lambda i, got: first_pair(c * CHP + i, got), carry, unroll=4
+            0, CHP // GROUP, lambda i, got: scatter_group(c * (CHP // GROUP) + i, got), carry
         )
 
-    lax.fori_loop(0, CHUNKS, first_chunk, 0)
+    lax.fori_loop(0, PAIRS, build_pair, 0, unroll=4)
+    lax.fori_loop(0, EARLY, first_chunk, 0)
+    for c in range(EARLY, CHUNKS):
+        chunk_copy(c).wait()
 
     def take_extra(i, carry):
         blk_ids = [swap_ref[0, 2 * i + b] for b in range(2)]
         for b in range(2):
             w_ref[PB + 2 * i + b] = w_ref[blk_ids[b]]
-        for ref in (s0_ref, s1_ref, m_ref, sf_ref):
+        for ref in (s0_ref, s1_ref, m0_ref, m1_ref, f0_ref, f1_ref):
             vals = []
             for b in range(2):
                 v = ref[lax.div(blk_ids[b], 2)]
@@ -302,21 +300,17 @@
         return carry
 
     lax.fori_loop(0, XPAIRS, take_extra, 0)
-    lax.fori_loop(PAIRS, ALLP, next_scatter, 0, unroll=2)
+    lax.fori_loop(NAT, ALLP // GROUP, scatter_group, 0)
 
     def channels(first, count, groups):
         lo_c = iota((count, 128), 1) < 64
-
-        def folded(c):
-            v = pt_ref[pl.ds(first * 8 + c, count, stride=8), :]
-            return v + pltpu.roll(v, 64, 1)
-
+        v = [pt_ref[pl.ds(first * 8 + c, count, stride=8), :] for c in range(8)]
         parts = [
-            jnp.where(lo_c, folded(0), folded(1)),
-            jnp.where(lo_c, folded(2), folded(3)),
+            jnp.where(lo_c, v[0], v[6]) + pltpu.roll(jnp.where(lo_c, v[1], v[5]), 64, 1),
+            jnp.where(lo_c, v[2], 0.0) + pltpu.roll(jnp.where(lo_c, v[3], v[7]), 64, 1),
         ]
         if groups > 2:
-            parts.append(folded(4))
+            parts.append(v[4])
         return parts
 
     tgt = tgt_ref[...].astype(f32)
@@ -346,6 +340,7 @@
     hand1 = partner_copies(hs1, hr1, 0)
     for c in hand1:
         c.start()
+    lax.fori_loop(EARLY * CHP // GROUP, NAT, scatter_group, 0)
 
     own_cols = []
     for j in range(3):
@@ -392,14 +387,12 @@
         main = jnp.where(first_half, res[:, 0:128], res[:, 128:256])
         return main.reshape(16, 8, 128), res[:, 256:]
 
-    def fill1(c, carry):
+    def fill1(c):
         main, extra = send_rows(c, 3)
         owners = pl.ds(pl.multiple_of(c * 16, 16), 16)
         send1[owners] = jnp.concatenate([main, extra.reshape(16, 8, 128)], 1).astype(bf16)
-        return carry
-
-    lax.fori_loop(0, 8, fill1, 0)
-    all_to_all(send1, recv1, 0)
+
+    all_to_all(fill1, send1, recv1, 0)
 
     key_lane = iota((EXT, 128), 1)
     for c in range(8):
@@ -449,18 +442,23 @@
         rest = jnp.where(keep1, total[NBD:, 128:256] / msafe, 0.0)
         return jnp.concatenate([vel, rest], 1).astype(bf16)
 
-    def answer(fields, dst):
+    def answer(fields, ph):
         rhs = jnp.concatenate([jnp.zeros((NBD, 256), bf16), fields], 0)
 
-        def fill(c, carry):
+        def fill(c):
             rows = pl.ds(pl.multiple_of(c * 128, 128), 128)
             res = dot(at_ref[rows, :], rhs)
             main = jnp.where(half0, res[:, 0:128], res[:, 128:256])
             owners = pl.ds(pl.multiple_of(c * 16, 16), 16)
-            dst[owners] = main.reshape(16, 8, 128).astype(bf16)
-            return carry
-
-        lax.fori_loop(0, 8, fill, 0)
+            ans_s[ph, owners] = main.reshape(16, 8, 128).astype(bf16)
+
+        all_to_all(fill, ans_s.at[ph], ans_r.at[ph], 1 + 2 * ph)
+
+    def put_fields(first, count, fields):
+        flat = fbx_ref.reshape(EXT * 8, 128)
+        a, b = fields[0:count, 0:128], fields[0:count, 128:256]
+        for g, val in enumerate((a, b, pltpu.roll(a, 64, 1), pltpu.roll(b, 64, 1))):
+            flat[pl.ds(first * 8 + g, count, stride=8), :] = val
 
     def spread(src, ph):
         total = jnp.zeros((EXT, 256), f32)
@@ -475,18 +473,14 @@
         copies = partner_copies(fs.at[ph], fr.at[ph], 1 + ph)
         for c in copies:
             c.start()
-        fbx_ref[0:PB, 0:256] = total[0:PB]
-        fbx_ref[0:PB, 256:384] = pltpu.roll(total[0:PB, 0:128], 64, 1)
-        fbx_ref[0:PB, 384:512] = pltpu.roll(total[0:PB, 128:256], 64, 1)
+        put_fields(0, PB, total)
         return copies
 
     def spread_end(copies, ph):
         for c in copies:
             c.wait()
         got = picked(fr.at[ph])
-        fbx_ref[PB : PB + SWP, 0:256] = got
-        fbx_ref[PB : PB + SWP, 256:384] = pltpu.roll(got[:, 0:128], 64, 1)
-        fbx_ref[PB : PB + SWP, 384:512] = pltpu.roll(got[:, 128:256], 64, 1)
+        put_fields(PB, SWP, got)
 
     total = grid_sum1(0)
     for c in range(1, 8):
@@ -494,19 +488,18 @@
     mass_n = total[NBD:, 256:384]
     msafe = jnp.maximum(jnp.where(lane_n < 64, mass_n, pltpu.roll(mass_n, 64, 1)), 0.25)
     ms_ref[...] = msafe
-    answer(grid_fields(total, msafe), ans_s.at[0])
-    all_to_all(ans_s.at[0], ans_r.at[0], 1)
+    answer(grid_fields(total, msafe), 0)
     all_to_all_wait(ans_s.at[0], ans_r.at[0], 1)
 
     copies = spread(ans_r.at[0], 0)
-    lax.fori_loop(0, 24, middle_four, 0)
+    lax.fori_loop(0, NAT // 2, middle_group, 0)
     spread_end(copies, 0)
-    lax.fori_loop(PAIRS // 4, ALLP // 4, middle_four, 0)
+    lax.fori_loop(NAT, ALLP // GROUP, middle_group, 0)
     hs2[...] = jnp.concatenate(channels(PB, SWP, 2), 1).astype(bf16)
     hand2 = partner_copies(hs2, hr2, 3)
     for c in hand2:
         c.start()
-    lax.fori_loop(24, PAIRS // 4, middle_four, 0)
+    lax.fori_loop(NAT // 2, NAT, middle_group, 0)
     for j in range(3):
         pb_ref[j * 128 : j * 128 + 128, 0:256] = jnp.concatenate(
             channels(j * 128, 128, 2), 1
@@ -515,31 +508,28 @@
         c.wait()
     pb_ref[PB : PB + SWP, 0:256] = picked(hr2).astype(bf16)
 
-    def fill2(c, carry):
+    def fill2(c):
         main, _ = send_rows(c, 2)
         send2[pl.ds(pl.multiple_of(c * 16, 16), 16)] = main.astype(bf16)
-        return carry
-
-    lax.fori_loop(0, 8, fill2, 0)
-    all_to_all(send2, recv2, 2)
+
+    all_to_all(fill2, send2, recv2, 2)
     all_to_all_wait(send2, recv2, 2)
     total = grid_sum2(0)
     for c in range(1, 8):
         total = total + grid_sum2(c)
     fields = grid_fields(total, ms_ref[...])
     field_ref[...] = fields
-    answer(fields, ans_s.at[1])
-    all_to_all(ans_s.at[1], ans_r.at[1], 3)
+    answer(fields, 1)
     all_to_all_wait(ans_s.at[1], ans_r.at[1], 3)
 
     copies = spread(ans_r.at[1], 1)
-    lax.fori_loop(0, 24, last_four, 0)
+    lax.fori_loop(0, NAT // 2, last_group, 0)
     spread_end(copies, 1)
-    lax.fori_loop(PAIRS // 4, ALLP // 4, last_extra, 0)
+    lax.fori_loop(NAT, ALLP // GROUP, last_extra, 0)
     hand3 = partner_copies(xs, xr, 4)
     for c in hand3:
         c.start()
-    lax.fori_loop(24, PAIRS // 4, last_four, 0)
+    lax.fori_loop(NAT // 2, NAT, last_group, 0)
     for c in hand3:
         c.wait()
     xout_ref[...] = picked(xr)
@@ -564,9 +554,11 @@
             pltpu.VMEM((ALLP, 8, 128), f32),
             pltpu.VMEM((ALLP, 8, 128), f32),
             pltpu.VMEM((ALLP, 8, 128), f32),
+            pltpu.VMEM((ALLP, 8, 128), f32),
+            pltpu.VMEM((ALLP, 8, 128), f32),
             pltpu.VMEM((EXT * 8, 128), f32),
             pltpu.VMEM((EXT, 384), bf16),
-            pltpu.VMEM((EXT, 512), f32),
+            pltpu.VMEM((EXT, 8, 128), f32),
             pltpu.VMEM((EXT, 128), f32),
             pltpu.VMEM((128, EXT), f32),
             pltpu.VMEM((EXT, ROWS), bf16),

time: 106 us -> 84.8 us (0.80)
  Pallas kernels: 101 us -> 80.4 us
    pallas_call x1, Pallas kernels: 97.6 us -> 76.9 us  [weld_call(): pl.pallas_call(weld_kernel, out_shape=(jax.ShapeDtypeStruct((10, PB * BS)...]
where the time goes in v1:
time: 84.8 us; the launch traced here: 84.6 us
  Pallas kernels  80.4 us (95%)
  local copies, waits for them, and re-layouts  2.92 us (3%)
  between operations  1.31 us (2%)
    pallas_call x1, Pallas kernels, weld_call(): pl.pallas_call(weld_kernel, out_shape=(jax.ShapeDtypeStruct((10, PB * BS)...  76.9 us
    pallas_call x1, Pallas kernels, place_call(): pl.pallas_call(place_kernel, out_shape=jax.ShapeDtypeStruct((10, PB * BS)...  3.54 us
    unnamed x9, local copies, waits for them, and re-layouts  2.92 us

profile of v1, /device:TPU:1, one launch (start us, length us, event | category | flops | bytes accessed | tf_op | source)
XLA Modules:
  0.0 84.6 jit_solution(12599879230719887398)
XLA Ops:
  1.3 0.0 copy-start.2
  1.3 76.9 %shard_map.95 = (f32[10,24576]{1,0:T(8,128)}, bf16[64,256]{1,0:T(8,128)(2,1)}, f32[16,1536]{1,0:T(8,128)}) custom-call(bf16[384,64,256]{2,1,0:T(8,128)(2,1)} %w_hbm.1, f32[10,24576]{1,0:T(8,128)} %st_ref.1, f32[1,24576]{1,0:T(1,128)} %bitcast.3, f32[1,24576]{1,0:T(1,128)} %bitcast.4, s32[3,128]{1,0:T(4,128)} %bitcast.5, s32[384]{0:T(512)} %cnt_ref.1, ...), custom_call_target="tpu_custom_call" | custom-call | tf_op jit(solution)/shard_map/pallas_call | solution.py:542
  78.2 0.0 copy-done.2
  78.2 0.0 copy-start
  78.2 1.4 %copy-done = f32[10,24576]{1,0:T(8,128)S(1)} copy-done((f32[10,24576]{1,0:T(8,128)S(1)}, f32[10,24576]{1,0:T(8,128)}, u32[]{:S(2)}) %copy-start) | copy-done | bytes 983064
  79.6 0.0 copy-start.1
  79.6 0.9 %copy-done.1 = f32[16,1536]{1,0:T(8,128)S(1)} copy-done((f32[16,1536]{1,0:T(8,128)S(1)}, f32[16,1536]{1,0:T(8,128)}, u32[]{:S(2)}) %copy-start.1) | copy-done | bytes 98328
  80.5 0.0 copy-start.3
  80.5 3.5 %shard_map.96 = f32[10,24576]{1,0:T(8,128)} custom-call(f32[10,24576]{1,0:T(8,128)S(1)} %copy-done, f32[16,1536]{1,0:T(8,128)S(1)} %copy-done.1, s32[1,24]{1,0:T(1,128)S(1)} %copy-done.2), custom_call_target="tpu_custom_call" | custom-call | tf_op jit(solution)/shard_map/pallas_call | solution.py:616
  84.0 0.0 copy-done.3
  84.0 0.6 copy.12
Async XLA Ops:
  1.3 76.9 %copy-start.2 = (s32[1,24]{1,0:T(1,128)S(1)}, s32[1,24]{1,0:T(1,128)}, u32[]{:S(2)}) copy-start(s32[1,24]{1,0:T(1,128)} %swap_ref.3) | copy-start | bytes 292
  78.2 1.4 %copy-start = (f32[10,24576]{1,0:T(8,128)S(1)}, f32[10,24576]{1,0:T(8,128)}, u32[]{:S(2)}) copy-start(f32[10,24576]{1,0:T(8,128)} %get-tuple-element.5.own_ref) | copy-start | bytes 2949124
  79.6 0.9 %copy-start.1 = (f32[16,1536]{1,0:T(8,128)S(1)}, f32[16,1536]{1,0:T(8,128)}, u32[]{:S(2)}) copy-start(f32[16,1536]{1,0:T(8,128)} %get-tuple-element.6.got_ref) | copy-start | bytes 294916
  80.5 3.5 %copy-start.3 = (bf16[64,256]{1,0:T(8,128)(2,1)S(1)}, bf16[64,256]{1,0:T(8,128)(2,1)}, u32[]{:S(2)}) copy-start(bf16[64,256]{1,0:T(8,128)(2,1)} %get-tuple-element.11) | copy-start | bytes 98308

commit v2 on v1

--- a/solution.py
+++ b/solution.py
@@ -85,11 +85,11 @@
 
     def all_to_all(fill, src, dst, ph):
         def row(i, carry):
-            w = lax.rem(weld + i, N_WELD)
+            w = lax.rem(weld + N_WELD // 2 + i, N_WELD)
             fill(w)
 
             def go(j, inner):
-                t = lax.rem(trans + j, N_TRANS)
+                t = lax.rem(trans + N_TRANS // 2 + j, N_TRANS)
                 dev = w * N_TRANS + t
 
                 @pl.when(dev != me)
@@ -101,7 +101,7 @@
 
                 return inner
 
-            lax.fori_loop(0, N_TRANS, go, 0)
+            lax.fori_loop(0, N_TRANS, go, 0, unroll=4)
             return carry
 
         lax.fori_loop(0, N_WELD, row, 0)
@@ -143,7 +143,7 @@
     def scatter_put(q, res):
         pt_ref[pl.ds(pl.multiple_of(q * 16, 16), 16), :] = res
 
-    def build_pair(q, carry):
+    def build_pair(q):
         lanes = pl.ds(pl.multiple_of(q * 128, 128), 128)
 
         def row(r):
@@ -159,12 +159,23 @@
         live = lane64 < many
         mass8 = jnp.where(live, jnp.broadcast_to(mass_ref[0:1, lanes], (8, 128)), 0.0)
         stiff8 = jnp.where(live, 0.25 * jnp.broadcast_to(stiff_ref[0:1, lanes], (8, 128)), 0.0)
-        s0_ref[q] = s0
-        s1_ref[q] = s1
-        m0_ref[q] = jnp.where(row8 < 5, mass8, -0.25 * mass8)
-        m1_ref[q] = -0.25 * mass8
-        f0_ref[q] = jnp.where(row8 < 5, 0.0, stiff8)
-        f1_ref[q] = jnp.where(gap, 0.0, stiff8)
+        return (
+            s0,
+            s1,
+            jnp.where(row8 < 5, mass8, -0.25 * mass8),
+            -0.25 * mass8,
+            jnp.where(row8 < 5, 0.0, stiff8),
+            jnp.where(gap, 0.0, stiff8),
+        )
+
+    tile_refs = (s0_ref, s1_ref, m0_ref, m1_ref, f0_ref, f1_ref)
+
+    def build_group(g, carry):
+        group = [4 * g + p for p in range(4)]
+        built = [build_pair(q) for q in group]
+        for q, tiles in zip(group, built):
+            for ref, tile in zip(tile_refs, tiles):
+                ref[q] = tile
         return carry
 
     def scatter_group(g, carry):
@@ -282,7 +293,7 @@
             0, CHP // GROUP, lambda i, got: scatter_group(c * (CHP // GROUP) + i, got), carry
         )
 
-    lax.fori_loop(0, PAIRS, build_pair, 0, unroll=4)
+    lax.fori_loop(0, PAIRS // 4, build_group, 0)
     lax.fori_loop(0, EARLY, first_chunk, 0)
     for c in range(EARLY, CHUNKS):
         chunk_copy(c).wait()
@@ -291,7 +302,7 @@
         blk_ids = [swap_ref[0, 2 * i + b] for b in range(2)]
         for b in range(2):
             w_ref[PB + 2 * i + b] = w_ref[blk_ids[b]]
-        for ref in (s0_ref, s1_ref, m0_ref, m1_ref, f0_ref, f1_ref):
+        for ref in tile_refs:
             vals = []
             for b in range(2):
                 v = ref[lax.div(blk_ids[b], 2)]
@@ -299,7 +310,7 @@
             ref[PAIRS + i] = jnp.where(lo, vals[0], vals[1])
         return carry
 
-    lax.fori_loop(0, XPAIRS, take_extra, 0)
+    lax.fori_loop(0, XPAIRS, take_extra, 0, unroll=4)
     lax.fori_loop(NAT, ALLP // GROUP, scatter_group, 0)
 
     def channels(first, count, groups):
@@ -591,13 +602,21 @@
     )(weights, state, mass, stiff, targets, counts, bit, swap)
 
 
-def place_kernel(own_ref, got_ref, swap_ref, out_ref):
-    out_ref[...] = own_ref[...]
+def place_kernel(own_hbm, got_hbm, fields_hbm, swap_ref, out_ref, fields_out, got_ref, sem):
+    copies = [
+        pltpu.make_async_copy(src, dst, sem.at[i])
+        for i, (src, dst) in enumerate(
+            ((own_hbm, out_ref), (got_hbm, got_ref), (fields_hbm, fields_out))
+        )
+    ]
+    for c in copies:
+        c.start()
     lane = iota((8, 128), 1)
-
-    def place(s, carry):
+    for c in copies:
+        c.wait()
+    for s in range(SW):
         blk_id = swap_ref[0, s]
-        src = pl.ds(pl.multiple_of((s // 2) * 128, 128), 128)
+        src = slice((s // 2) * 128, (s // 2) * 128 + 128)
         dst = pl.ds(pl.multiple_of((blk_id // 2) * 128, 128), 128)
         same = (s % 2) == (blk_id % 2)
         mine = (lane >= 64) == (blk_id % 2 == 1)
@@ -606,20 +625,25 @@
         low = jnp.where(same, low, pltpu.roll(low, 64, 1))
         out_ref[0:8, dst] = jnp.where(mine, top, out_ref[0:8, dst])
         out_ref[8:10, dst] = jnp.where(mine[0:2], low[0:2], out_ref[8:10, dst])
-        return carry
-
-    lax.fori_loop(0, SW, place, 0)
-
-
-def place_call(own, got, swap):
+
+
+def place_call(own, got, fields, swap):
     vmem = pl.BlockSpec(memory_space=pltpu.VMEM)
+    hbm = pl.BlockSpec(memory_space=pl.ANY)
     return pl.pallas_call(
         place_kernel,
-        out_shape=jax.ShapeDtypeStruct((10, PB * BS), f32),
-        in_specs=[vmem, vmem, pl.BlockSpec(memory_space=pltpu.SMEM)],
-        out_specs=vmem,
-        compiler_params=pltpu.CompilerParams(vmem_limit_bytes=32 * 1024 * 1024),
-    )(own, got, swap)
+        out_shape=(
+            jax.ShapeDtypeStruct((10, PB * BS), f32),
+            jax.ShapeDtypeStruct((NBD, 4 * BS), bf16),
+        ),
+        in_specs=[hbm, hbm, hbm, pl.BlockSpec(memory_space=pltpu.SMEM)],
+        out_specs=(vmem, hbm),
+        scratch_shapes=[
+            pltpu.VMEM((16, XPAIRS * 128), f32),
+            pltpu.SemaphoreType.DMA((3,)),
+        ],
+        compiler_params=pltpu.CompilerParams(vmem_limit_bytes=56 * 1024 * 1024),
+    )(own, got, fields, swap)
 
 
 def shards(weights, particle_state, mass, stiffness, targets, counts, partner_bit, swap_list):
@@ -633,7 +657,7 @@
         partner_bit,
         swap_list,
     )
-    return place_call(own, got, swap_list), fields
+    return place_call(own, got, fields, swap_list)
 
 
 def solution(mesh):

time: 84.8 us -> 79.4 us (0.936)
  local copies, waits for them, and re-layouts: 2.92 us -> 0 us
  Pallas kernels: 80.4 us -> 78 us
    pallas_call x1, Pallas kernels: 76.9 us -> 73.8 us  [weld_call(): pl.pallas_call(weld_kernel, out_shape=(jax.ShapeDtypeStruct((10, PB * BS)...]
    unnamed x9 -> x0, local copies, waits for them, and re-layouts: 2.92 us -> none
where the time goes in v2:
time: 79.4 us; the launch traced here: 79.2 us
  Pallas kernels  78 us (98%)
  between operations  1.29 us (2%)
    pallas_call x1, Pallas kernels, weld_call(): pl.pallas_call(weld_kernel, out_shape=(jax.ShapeDtypeStruct((10, PB * BS)...  73.8 us
    pallas_call x1, Pallas kernels, place_call(): pl.pallas_call(place_kernel, out_shape=(jax.ShapeDtypeStruct((10, PB * BS...  4.11 us

profile of v2, /device:TPU:1, one launch (start us, length us, event | category | flops | bytes accessed | tf_op | source)
XLA Modules:
  0.0 79.2 jit_solution(15310217415988711142)
XLA Ops:
  1.3 73.8 %shard_map.95 = (f32[10,24576]{1,0:T(8,128)}, bf16[64,256]{1,0:T(8,128)(2,1)}, f32[16,1536]{1,0:T(8,128)}) custom-call(bf16[384,64,256]{2,1,0:T(8,128)(2,1)} %w_hbm.1, f32[10,24576]{1,0:T(8,128)} %st_ref.1, f32[1,24576]{1,0:T(1,128)} %bitcast.3, f32[1,24576]{1,0:T(1,128)} %bitcast.4, s32[3,128]{1,0:T(4,128)} %bitcast.5, s32[384]{0:T(512)} %cnt_ref.1, ...), custom_call_target="tpu_custom_call" | custom-call | tf_op jit(solution)/shard_map/pallas_call | solution.py:553
  75.1 4.1 %shard_map.96 = (f32[10,24576]{1,0:T(8,128)}, bf16[64,256]{1,0:T(8,128)(2,1)}) custom-call(f32[10,24576]{1,0:T(8,128)} %get-tuple-element.5.own_hbm, f32[16,1536]{1,0:T(8,128)} %get-tuple-element.6.got_hbm, bf16[64,256]{1,0:T(8,128)(2,1)} %get-tuple-element.7.fields_hbm, s32[1,24]{1,0:T(1,128)} %swap_ref.3), custom_call_target="tpu_custom_call" | custom-call | tf_op jit(solution)/shard_map/pallas_call | solution.py:633

commit v3 on v2

--- a/solution.py
+++ b/solution.py
@@ -52,7 +52,7 @@
     w_hbm, st_ref, mass_ref, stiff_ref, tgt_ref, cnt_ref, bit_ref, swap_ref,
     out_ref, field_ref, xout_ref,
     w_ref, s0_ref, s1_ref, m0_ref, m1_ref, f0_ref, f1_ref, pt_ref, pb_ref, fbx_ref, kc_ref, kr_ref,
-    sd_ref, at_ref, a_ref, ms_ref,
+    sd_ref, pick_ref, at_ref, a_ref, ms_ref,
     send1, recv1, send2, recv2, ans_s, ans_r,
     hs1, hr1, hs2, hr2, fs, fr, xs, xr,
     wsem, asem_s, asem_r, hsem_s, hsem_r,
@@ -101,7 +101,7 @@
 
                 return inner
 
-            lax.fori_loop(0, N_TRANS, go, 0, unroll=4)
+            lax.fori_loop(0, N_TRANS, go, 0, unroll=8)
             return carry
 
         lax.fori_loop(0, N_WELD, row, 0)
@@ -390,9 +390,14 @@
         kr_ref[:, i * 128 : i * 128 + 128] = kc_ref[i * 128 : i * 128 + 128, :].T
 
     def send_rows(c, groups):
-        r = iota((128, EXT), 0) + c * 128
-        row_key = ((r // 8) * SLOTS + r % SLOTS).astype(f32)
-        pick = jnp.where(row_key == kr_ref[...], 1.0, 0.0).astype(bf16)
+        rows = pl.ds(pl.multiple_of(c * 128, 128), 128)
+        if groups == 3:
+            r = iota((128, EXT), 0) + c * 128
+            row_key = ((r // 8) * SLOTS + r % SLOTS).astype(f32)
+            pick = jnp.where(row_key == kr_ref[...], 1.0, 0.0).astype(bf16)
+            pick_ref[rows, :] = pick
+        else:
+            pick = pick_ref[rows, :]
         res = dot(pick, pb_ref[:, 0 : groups * 128])
         first_half = (iota((128, 128), 0) % 8) < SLOTS
         main = jnp.where(first_half, res[:, 0:128], res[:, 128:256])
@@ -472,18 +477,23 @@
             flat[pl.ds(first * 8 + g, count, stride=8), :] = val
 
     def spread(src, ph):
-        total = jnp.zeros((EXT, 256), f32)
+        parts = []
+        handed = jnp.zeros((SWP, 256), f32)
         for c in range(4):
             main = src[c * 32 : c * 32 + 32].astype(f32).reshape(256, 128)
             first_half = (iota((256, 128), 0) % 8) < SLOTS
             rhs = jnp.concatenate(
                 [jnp.where(first_half, main, 0.0), jnp.where(first_half, 0.0, main)], 1
             ).astype(bf16)
-            total = total + dot(sd_ref[:, c * 256 : c * 256 + 256], rhs)
-        fs[ph] = total[PB : PB + SWP].astype(bf16)
+            handed = handed + dot(sd_ref[PB : PB + SWP, c * 256 : c * 256 + 256], rhs)
+            parts.append(rhs)
+        fs[ph] = handed.astype(bf16)
         copies = partner_copies(fs.at[ph], fr.at[ph], 1 + ph)
         for c in copies:
             c.start()
+        total = jnp.zeros((PB, 256), f32)
+        for c in range(4):
+            total = total + dot(sd_ref[0:PB, c * 256 : c * 256 + 256], parts[c])
         put_fields(0, PB, total)
         return copies
 
@@ -573,6 +583,7 @@
             pltpu.VMEM((EXT, 128), f32),
             pltpu.VMEM((128, EXT), f32),
             pltpu.VMEM((EXT, ROWS), bf16),
+            pltpu.VMEM((ROWS, EXT), bf16),
             pltpu.VMEM((ROWS, 128), bf16),
             pltpu.VMEM((128, ROWS), bf16),
             pltpu.VMEM((NBD, 128), f32),

time: 79.4 us -> 79.3 us (level)
  no operation moved by 1% of the time
where the time goes in v3:
time: 79.3 us; the launch traced here: 79.1 us
  Pallas kernels  77.8 us (98%)
  between operations  1.29 us (2%)
    pallas_call x1, Pallas kernels, weld_call(): pl.pallas_call(weld_kernel, out_shape=(jax.ShapeDtypeStruct((10, PB * BS)...  73.7 us
    pallas_call x1, Pallas kernels, place_call(): pl.pallas_call(place_kernel, out_shape=(jax.ShapeDtypeStruct((10, PB * BS...  4.11 us

profile of v3, /device:TPU:1, one launch (start us, length us, event | category | flops | bytes accessed | tf_op | source)
XLA Modules:
  0.0 79.1 jit_solution(14783843752233621866)
XLA Ops:
  1.3 73.7 %shard_map.95 = (f32[10,24576]{1,0:T(8,128)}, bf16[64,256]{1,0:T(8,128)(2,1)}, f32[16,1536]{1,0:T(8,128)}) custom-call(bf16[384,64,256]{2,1,0:T(8,128)(2,1)} %w_hbm.1, f32[10,24576]{1,0:T(8,128)} %st_ref.1, f32[1,24576]{1,0:T(1,128)} %bitcast.3, f32[1,24576]{1,0:T(1,128)} %bitcast.4, s32[3,128]{1,0:T(4,128)} %bitcast.5, s32[384]{0:T(512)} %cnt_ref.1, ...), custom_call_target="tpu_custom_call" | custom-call | tf_op jit(solution)/shard_map/pallas_call | solution.py:563
  75.0 4.1 %shard_map.96 = (f32[10,24576]{1,0:T(8,128)}, bf16[64,256]{1,0:T(8,128)(2,1)}) custom-call(f32[10,24576]{1,0:T(8,128)} %get-tuple-element.5.own_hbm, f32[16,1536]{1,0:T(8,128)} %get-tuple-element.6.got_hbm, bf16[64,256]{1,0:T(8,128)(2,1)} %get-tuple-element.7.fields_hbm, s32[1,24]{1,0:T(1,128)} %swap_ref.3), custom_call_target="tpu_custom_call" | custom-call | tf_op jit(solution)/shard_map/pallas_call | solution.py:644
